TPU v7x, 32 devices: a whole 2x2x4 slice. The times are simulated.
32 devices in a mesh: grp: 2 (over y), run: 4 (over x, core), chan: 4 (over z).
Axes of the slice: x: 2, y: 2, z: 4, core: 2. Of those that a mesh axis runs over, the one named last changes fastest.
Arguments:
- embed: bfloat16 [512, 8192], P('grp', 'chan'), parts along dimension 0, may hold values from -6 to 6
- noise: bfloat16 [16, 32, 8192], P(('grp', 'run'), None, 'chan'), parts along dimension 0, may hold values from -12 to 12
- positions: int32 [16, 32], P(('grp', 'run')), parts along dimension 0, may hold values from 0 to 255
- restore: int32 [16, 2], P(('grp', 'run')), parts along dimension 0, may hold values 0 or 1
- short_one: float32 [7, 8192], P(None, 'chan'), may hold values from -2 to 2
- long_one: float32 [128, 8192], P(None, 'chan'), may hold values from -0.5 to 0.5
- out_weight: bfloat16 [8192, 8192], P(None, 'chan'), may hold values from -0.0625 to 0.0625
- short_two: float32 [7, 8192], P(None, 'chan'), may hold values from -2 to 2
- long_two: float32 [128, 8192], P(None, 'chan'), may hold values from -0.5 to 0.5
Outputs:
- traced: bfloat16 [16, 256, 8192], P(('grp', 'run'), None, 'chan'), parts along dimension 0
There are 2 independent parts, one for each index of `grp`. A program takes and returns all parts, laid end to end along the dimension named above; an argument that names none is the same for every part. Nothing has to cross between parts.
All inputs are finite; a program needn't handle non-finite values. No bound on the sum of `restore` on one device may be relied on, other than what follows from the above.
Results may differ from a plain program's by a relative error of at most 0.007.
Values may be sent and summed in bfloat16 or wider, within the bound.
A program may use at most 128 MiB of HBM per device.

v0:
```python
import jax
import jax.numpy as jnp
from jax import lax
from jax.sharding import PartitionSpec as P


def short_filter(field, filter_taps):
    length = field.shape[1]
    running = jnp.zeros(field.shape, jnp.float32)
    for shift_count in range(filter_taps.shape[0]):
        shifted = jnp.pad(field, ((0, 0), (shift_count, 0), (0, 0)))[:, :length]
        running = running + filter_taps[shift_count][None, None, :] * shifted
    return running


def block_filter(field, filter_taps):
    width = field.shape[2]
    span = filter_taps.shape[0]
    kernel = filter_taps[::-1][:, None, :]
    return lax.conv_general_dilated(
        field,
        kernel,
        window_strides=(1,),
        padding=((span - 1, 0),),
        dimension_numbers=("NWC", "WIO", "NWC"),
        feature_group_count=width,
        precision=lax.Precision.HIGHEST,
        preferred_element_type=jnp.float32,
    )


def per_device(
    embed, noise, positions, restore, short_one, long_one, out_weight, short_two, long_two
):
    run_count = noise.shape[0]
    length = embed.shape[0]
    first_run = lax.axis_index("run") * run_count
    run_ids = first_run + jnp.arange(run_count, dtype=jnp.int32)
    onehot = (jnp.arange(length, dtype=jnp.int32)[None, :, None] == positions[:, None, :]).astype(
        jnp.bfloat16
    )
    added = jnp.einsum("rlp,rpc->rlc", onehot, noise, preferred_element_type=jnp.float32)
    corrupt_flag = (run_ids != 0).astype(jnp.float32)[:, None, None]
    inputs = (embed.astype(jnp.float32)[None] + corrupt_flag * added).astype(jnp.bfloat16)
    batch_inputs = jnp.concatenate([inputs, embed[None]], axis=0)
    input_values = batch_inputs.astype(jnp.float32)
    filtered = block_filter(short_filter(input_values, short_one), long_one)
    mixed = (filtered * jax.nn.silu(input_values)).astype(jnp.bfloat16)
    initial = jnp.zeros((mixed.shape[0], length, out_weight.shape[1]), jnp.float32)
    segment = lax.all_gather(mixed, "chan", axis=2, tiled=True)
    weight_rows = lax.slice_in_dim(out_weight, 0, segment.shape[2], axis=0)
    projected = initial + jnp.einsum(
        "rlk,kc->rlc", segment, weight_rows, preferred_element_type=jnp.float32
    )
    hidden = (input_values + projected).astype(jnp.bfloat16)
    clean_hidden = hidden[run_count]
    hidden = hidden[:run_count]
    block_size = length // restore.shape[1]
    restored_rows = jnp.repeat(restore, block_size, axis=1)[:, :, None] == 1
    restored = jnp.where(restored_rows, clean_hidden[None], hidden)
    restored_values = restored.astype(jnp.float32)
    second = block_filter(short_filter(restored_values, short_two), long_two)
    return (restored_values + second * jax.nn.silu(restored_values)).astype(jnp.bfloat16)


def solution(mesh):
    in_specs = (
        P("grp", "chan"),
        P(("grp", "run"), None, "chan"),
        P(("grp", "run"), None),
        P(("grp", "run"), None),
        P(None, "chan"),
        P(None, "chan"),
        P(None, "chan"),
        P(None, "chan"),
        P(None, "chan"),
    )
    out_specs = P(("grp", "run"), None, "chan")
    return jax.shard_map(
        per_device, mesh=mesh, in_specs=in_specs, out_specs=out_specs, check_vma=False
    )
```

profile of v0, /device:TPU:0, one launch (start us, length us, event | category | flops | bytes accessed | tf_op | source)
XLA Modules:
  0.0 446.8 jit_solution(15623138889471099007)
XLA Ops:
  6.5 0.0 copy-start
  6.5 0.0 copy-start.6
  6.5 0.0 all-gather.2.cloned.1.call-start
  6.5 1.2 fusion.40
  7.8 0.0 copy-start.2
  7.8 2.9 convert_element_type.53
  10.7 8.9 %rev.6 = f32[128,2048]{1,0:T(8,128)} reverse(f32[128,2048]{1,0:T(8,128)} %param.14), dimensions={0} | reverse | bytes 2097152 | tf_op jit(solution)/shard_map/rev | solution.py:19
  19.5 0.0 copy-done
  19.5 0.0 copy-done.6
  19.5 2.4 add_convert_fusion.1
  22.0 0.0 copy-done.2
  22.0 0.4 maximum_convert_fusion
  22.4 0.0 copy-start.4
  22.4 5.2 %fusion.10 = f32[3,256,2048]{2,1,0:T(8,128)S(1)} fusion(f32[3,256,2048]{2,1,0:T(8,128)S(1)} %maximum_convert_fusion, f32[2048]{0:T(1024)S(1)} %bitcast.48, f32[2048]{0:T(1024)S(1)} %bitcast.49, f32[2048]{0:T(1024)S(1)} %bitcast.44, f32[2048]{0:T(1024)S(1)} %bitcast.45, f32[2048]{0:T(1024)S(1)} %bitcast.46, f32[2048]{0:T(1024)S(1)} %bitcast.47, ...), kind=kLoop, calls=%fused_computation.16 | loop fusion | flops 20447232 | bytes 12640256 | tf_op jit(solution)/shard_map/add | solution.py:12
  27.6 0.0 copy-done.4
  27.6 98.9 %fusion.2 = f32[3,256,2048]{2,0,1:T(4,128)S(1)} fusion(f32[3,256,2048]{2,1,0:T(8,128)S(1)} %fusion.10, f32[128,1,2048]{2,0,1:T(8,128)S(1)} %bitcast.35), kind=kOutput, calls=%fused_computation.2 | convolution fusion | flops 1816657920 | bytes 13631488 | tf_op jit(solution)/shard_map/conv_general_dilated | solution.py:20
  126.5 0.0 copy-start.7
  126.5 5.2 %fusion.16 = bf16[3,256,2048]{2,1,0:T(8,128)(2,1)} fusion(f32[3,256,2048]{2,0,1:T(4,128)S(1)} %fusion.2, bf16[1,256,2048]{2,1,0:T(8,128)(2,1)S(1)} %bitcast.32, bf16[2,256,2048]{2,1,0:T(8,128)(2,1)S(1)} %add_convert_fusion.1), kind=kLoop, calls=%fused_computation.23 | loop fusion | flops 12582912 | bytes 12582912 | tf_op jit(solution)/shard_map/convert_element_type | solution.py:48
  131.7 0.0 copy-start.5
  131.7 0.0 all-gather.2.cloned.1.call-update
  131.8 0.0 copy-done.7
  131.8 0.1 broadcast_bitcast_fusion
  131.9 8.9 %rev.7 = f32[128,2048]{1,0:T(8,128)} reverse(f32[128,2048]{1,0:T(8,128)} %param.17), dimensions={0} | reverse | bytes 2097152 | tf_op jit(solution)/shard_map/rev | solution.py:19
  140.7 0.0 copy-done.5
  140.8 212.0 %all-gather.2.cloned.1.call-done = bf16[3,256,8192]{2,1,0:T(8,128)(2,1)} async-done(((bf16[3,256,2048]{2,1,0:T(8,128)(2,1)}), bf16[3,256,8192]{2,1,0:T(8,128)(2,1)}) %all-gather.2.cloned.1.call-update) | async-done | bytes 12582928 | tf_op jit(solution)/shard_map/all_gather | solution.py:50
  352.8 33.6 %add_convert_fusion = bf16[3,256,2048]{2,1,0:T(8,128)(2,1)S(1)} fusion(bf16[3,256,8192]{2,1,0:T(8,128)(2,1)} %all-gather.2.cloned.1.call-done, bf16[8192,2048]{1,0:T(8,128)(2,1)} %param.15, bf16[1,256,2048]{2,1,0:T(8,128)(2,1)S(1)} %bitcast.33, bf16[2,256,2048]{2,1,0:T(8,128)(2,1)S(1)} %add_convert_fusion.1), kind=kOutput, calls=%fused_computation.24 | convolution fusion | flops 25776095232 | bytes 52428800 | tf_op jit(solution)/shard_map/rlk,kc->rlc/dot_general | solution.py:52
  386.5 0.1 slice_bitcast_fusion
  386.6 0.4 fusion.35
  386.9 0.0 copy-start.3
  386.9 3.5 fusion.23
  390.4 0.0 copy-done.3
  390.4 0.0 copy-start.1
  390.4 45.4 %fusion.31 = f32[2,256,2048]{2,0,1:T(2,128)S(1)} fusion(f32[2,256,2048]{2,1,0:T(8,128)S(1)} %fusion.23, f32[128,1,2048]{2,0,1:T(8,128)S(1)} %bitcast.34), kind=kOutput, calls=%fused_computation.46 | convolution fusion | flops 1211105280 | bytes 9437184 | tf_op jit(solution)/shard_map/conv_general_dilated | solution.py:20
  435.9 4.1 fusion.30
  439.9 0.0 copy-done.1
  (4 shorter events, 0.1 us)
Async XLA Ops:
  6.5 13.0 %copy-start = (bf16[2,32,2048]{2,1,0:T(8,128)(2,1)S(1)}, bf16[2,32,2048]{2,1,0:T(8,128)(2,1)}, u32[]{:S(2)}) copy-start(bf16[2,32,2048]{2,1,0:T(8,128)(2,1)} %param.10) | copy-start | bytes 786436
  6.5 13.0 %copy-start.6 = (s32[2,32]{1,0:T(2,128)S(1)}, s32[2,32]{1,0:T(2,128)}, u32[]{:S(2)}) copy-start(s32[2,32]{1,0:T(2,128)} %param.11) | copy-start | bytes 772
  6.5 346.3 %all-gather.2.cloned.1.call-start = ((), (), s32[]{:S(2)}) async-start(), calls=%async_computation | async-start | bytes 15728640 | tf_op jit(solution)/shard_map/all_gather | solution.py:50
  7.8 14.2 %copy-start.2 = (bf16[256,2048]{1,0:T(8,128)(2,1)S(1)}, bf16[256,2048]{1,0:T(8,128)(2,1)}, u32[]{:S(2)}) copy-start(bf16[256,2048]{1,0:T(8,128)(2,1)} %param.9) | copy-start | bytes 3145732
  22.4 5.2 %copy-start.4 = (f32[128,2048]{1,0:T(8,128)S(1)}, f32[128,2048]{1,0:T(8,128)}, u32[]{:S(2)}) copy-start(f32[128,2048]{1,0:T(8,128)} %rev.6) | copy-start | bytes 3145732
  126.5 5.3 %copy-start.7 = (s32[2,2]{1,0:T(2,128)S(1)}, s32[2,2]{1,0:T(2,128)}, u32[]{:S(2)}) copy-start(s32[2,2]{1,0:T(2,128)} %param.12) | copy-start | bytes 52
  131.7 9.0 %copy-start.5 = (f32[7,2048]{1,0:T(8,128)S(1)}, f32[7,2048]{1,0:T(8,128)}, u32[]{:S(2)}) copy-start(f32[7,2048]{1,0:T(8,128)} %param.16) | copy-start | bytes 172036
  386.9 3.5 copy-start.3
  390.4 49.5 %copy-start.1 = (bf16[2,32,2048]{2,1,0:T(8,128)(2,1)S(1)}, bf16[2,32,2048]{2,1,0:T(8,128)(2,1)}, u32[]{:S(2)}) copy-start(bf16[2,32,2048]{2,1,0:T(8,128)(2,1)} %param.10) | copy-start | bytes 786436
Sparse Core Ops, SparseCore 0:
  131.9 220.8 all-gather.1
where the time goes:
time: 448 us; the launch traced here: 447 us
  waiting for transfers between devices  212 us (47%)
  matrix products  180 us (40%)
  other arithmetic  21.6 us (5%)
  local copies, waits for them, and re-layouts  19.2 us (4%)
  between operations  13.6 us (3%)
    all_gather x1, waiting for transfers between devices, per_device(): segment = lax.all_gather(mixed, 'chan', axis=2, tiled=True)  212 us
    conv_general_dilated x2, matrix products, block_filter(): lax.conv_general_dilated(field, kernel, window_strides=(1,), padding=((sp...  144 us
    dot_general x1, matrix products, per_device(): jnp.einsum('rlk,kc->rlc', segment, weight_rows, preferred_element_type=jn...  33.6 us
    rev x2, local copies, waits for them, and re-layouts, block_filter(): kernel = filter_taps[::-1][:, None, :]  17.7 us
  transfers between devices with their start and end apart: 1, of which 1 were waited for; matrix products, arithmetic and copies ran while one was open for 2% of the time, Pallas kernels for 0%

commit v1 on v0

--- a/solution.py
+++ b/solution.py
@@ -47,7 +47,12 @@
     filtered = block_filter(short_filter(input_values, short_one), long_one)
     mixed = (filtered * jax.nn.silu(input_values)).astype(jnp.bfloat16)
     initial = jnp.zeros((mixed.shape[0], length, out_weight.shape[1]), jnp.float32)
-    segment = lax.all_gather(mixed, "chan", axis=2, tiled=True)
+    ring = [mixed]
+    for hop in range(3):
+        ring.append(lax.ppermute(ring[-1], "chan", [(dev, (dev + 1) % 4) for dev in range(4)]))
+    segment = jnp.roll(
+        jnp.concatenate(ring[::-1], axis=2), (lax.axis_index("chan") + 1) * ring[0].shape[2], axis=2
+    )
     weight_rows = lax.slice_in_dim(out_weight, 0, segment.shape[2], axis=0)
     projected = initial + jnp.einsum(
         "rlk,kc->rlc", segment, weight_rows, preferred_element_type=jnp.float32

time: 448 us -> 457 us (1.020)
  local copies, waits for them, and re-layouts: 19.2 us -> 45.9 us
  between operations: 13.6 us -> 0.21 us
  waiting for transfers between devices: 212 us -> 203 us
    all_gather x1 -> x0, waiting for transfers between devices: 212 us -> none  [per_device(): segment = lax.all_gather(mixed, 'chan', axis=2, tiled=True)]
    ppermute x0 -> x3, waiting for transfers between devices: none -> 203 us  [per_device(): lax.ppermute(ring[-1], 'chan', [(dev, (dev + 1) % 4) for dev in range(4)])]
    unnamed x18 -> x37, local copies, waits for them, and re-layouts: 0.12 us -> 24.9 us
    conv_general_dilated x2, matrix products: 144 us -> 149 us  [block_filter(): lax.conv_general_dilated(field, kernel, window_strides=(1,), padding=((sp...]
  transfers between devices with their start and end apart: 1 -> 3, of which waited for: 1 -> 3; matrix products, arithmetic and copies ran while one was open for 2% -> 2% of each run, Pallas kernels for 0% -> 0%
where the time goes in v1:
time: 457 us; the launch traced here: 456 us
  waiting for transfers between devices  203 us (44%)
  matrix products  184 us (40%)
  local copies, waits for them, and re-layouts  45.9 us (10%)
  other arithmetic  20.4 us (4%)
    ppermute x3, waiting for transfers between devices, per_device(): lax.ppermute(ring[-1], 'chan', [(dev, (dev + 1) % 4) for dev in range(4)])  203 us
    conv_general_dilated x2, matrix products, block_filter(): lax.conv_general_dilated(field, kernel, window_strides=(1,), padding=((sp...  149 us
    dot_general x1, matrix products, per_device(): jnp.einsum('rlk,kc->rlc', segment, weight_rows, preferred_element_type=jn...  33.7 us
    unnamed x37, local copies, waits for them, and re-layouts  24.9 us
    rev x2, local copies, waits for them, and re-layouts, block_filter(): kernel = filter_taps[::-1][:, None, :]  17.8 us
    add x2, other arithmetic, short_filter(): running = running + filter_taps[shift_count][None, None, :] * shifted  9.79 us
  transfers between devices with their start and end apart: 3, of which 3 were waited for; matrix products, arithmetic and copies ran while one was open for 2% of the time, Pallas kernels for 0%

profile of v1, /device:TPU:0, one launch (start us, length us, event | category | flops | bytes accessed | tf_op | source)
XLA Modules:
  0.0 455.9 jit_solution(7375964857474336920)
XLA Ops:
  0.0 0.0 copy-start
  0.0 0.0 copy-start.12
  0.0 1.2 fusion.44
  1.2 0.0 copy-start.6
  1.2 1.5 convert_element_type.53
  2.8 8.9 %rev.6 = f32[128,2048]{1,0:T(8,128)} reverse(f32[128,2048]{1,0:T(8,128)} %param.14), dimensions={0} | reverse | bytes 2097152 | tf_op jit(solution)/shard_map/rev | solution.py:19
  11.7 0.0 copy-done
  11.7 0.0 copy-done.12
  11.7 0.8 add_convert_fusion.1
  12.6 0.0 copy-start.2
  12.6 0.0 copy-done.6
  12.6 0.4 maximum_convert_fusion
  13.0 0.0 copy-start.10
  13.0 6.3 %fusion.11 = f32[3,256,2048]{2,1,0:T(8,128)} fusion(f32[3,256,2048]{2,1,0:T(8,128)S(1)} %maximum_convert_fusion, f32[2048]{0:T(1024)S(1)} %bitcast.47, f32[2048]{0:T(1024)S(1)} %bitcast.48, f32[2048]{0:T(1024)S(1)} %bitcast.43, f32[2048]{0:T(1024)S(1)} %bitcast.44, f32[2048]{0:T(1024)S(1)} %bitcast.45, f32[2048]{0:T(1024)S(1)} %bitcast.46, f32[2048]{0:T(1024)S(1)} %bitcast.42), kind=kLoop, calls=%fused_computation.17 | loop fusion | flops 20447232 | bytes 12640256 | tf_op jit(solution)/shard_map/add | solution.py:12
  19.4 0.0 copy-done.10
  19.4 0.0 copy-start.7
  19.4 103.7 %fusion.3 = f32[3,256,2048]{2,0,1:T(4,128)S(1)} fusion(f32[3,256,2048]{2,1,0:T(8,128)} %fusion.11, f32[128,1,2048]{2,0,1:T(8,128)S(1)} %bitcast.34), kind=kOutput, calls=%fused_computation.3 | convolution fusion | flops 1816657920 | bytes 13631488 | tf_op jit(solution)/shard_map/conv_general_dilated | solution.py:20
  123.1 0.0 copy-done.2
  123.1 0.0 copy-done.7
  123.1 0.0 copy-start.13
  123.1 0.0 copy-start.11
  123.1 4.1 fusion.17
  127.2 3.1 collective-permute-start
  130.3 70.1 %collective-permute-done = bf16[3,256,2048]{2,1,0:T(8,128)(2,1)S(1)} collective-permute-done((bf16[3,256,2048]{2,1,0:T(8,128)(2,1)S(1)}, bf16[3,256,2048]{2,1,0:T(8,128)(2,1)S(1)}, u32[]{:S(2)}, u32[]{:S(2)}) %collective-permute-start) | collective-permute-done | bytes 3145760 | tf_op jit(solution)/shard_map/ppermute | solution.py:52
  200.4 0.0 copy-start.4
  200.4 1.6 copy-done.4
  202.1 0.0 collective-permute-start.1
  202.1 71.2 %collective-permute-done.1 = bf16[3,256,2048]{2,1,0:T(8,128)(2,1)} collective-permute-done((bf16[3,256,2048]{2,1,0:T(8,128)(2,1)S(1)}, bf16[3,256,2048]{2,1,0:T(8,128)(2,1)}, u32[]{:S(2)}, u32[]{:S(2)}) %collective-permute-start.1) | collective-permute-done | bytes 3145760 | tf_op jit(solution)/shard_map/ppermute | solution.py:52
  273.3 0.0 collective-permute-start.2
  273.3 0.0 copy-done.13
  273.3 0.1 broadcast_bitcast_fusion
  273.4 8.9 %rev.7 = f32[128,2048]{1,0:T(8,128)} reverse(f32[128,2048]{1,0:T(8,128)} %param.17), dimensions={0} | reverse | bytes 2097152 | tf_op jit(solution)/shard_map/rev | solution.py:19
  282.2 0.0 copy-done.11
  282.3 61.5 %collective-permute-done.2 = bf16[3,256,2048]{2,1,0:T(8,128)(2,1)} collective-permute-done((bf16[3,256,2048]{2,1,0:T(8,128)(2,1)}, bf16[3,256,2048]{2,1,0:T(8,128)(2,1)}, u32[]{:S(2)}, u32[]{:S(2)}) %collective-permute-start.2) | collective-permute-done | bytes 3145760 | tf_op jit(solution)/shard_map/ppermute | solution.py:52
  343.7 4.0 constant_dynamic-update-slice_fusion.7
  347.7 0.0 copy-start.5
  347.7 4.1 constant_dynamic-update-slice_fusion.6
  351.8 0.0 copy-done.5
  351.8 2.1 constant_dynamic-update-slice_fusion.5
  353.9 1.9 constant_dynamic-update-slice_fusion.4
  355.7 3.9 constant_dynamic-update-slice_fusion.3
  359.7 3.9 constant_dynamic-update-slice_fusion.2
  363.6 2.1 constant_dynamic-update-slice_fusion.1
  365.7 0.0 copy-start.3
  365.7 0.0 copy-start.8
  365.7 1.9 constant_dynamic-update-slice_fusion
  367.6 0.7 copy-done.3
  368.3 0.4 copy-done.8
  368.7 33.7 %add_convert_fusion = bf16[3,256,2048]{2,1,0:T(8,128)(2,1)S(1)} fusion(bf16[8192,2048]{1,0:T(8,128)(2,1)} %param.15, bf16[3,256,16384]{2,1,0:T(8,128)(2,1)} %constant_dynamic-update-slice_fusion, s32[]{:T(128)S(6)} %select_n.18, bf16[1,256,2048]{2,1,0:T(8,128)(2,1)S(1)} %bitcast.32, bf16[2,256,2048]{2,1,0:T(8,128)(2,1)S(1)} %copy-done.3), kind=kOutput, calls=%fused_computation.25 | convolution fusion | flops 25776095232 | bytes 52428804 | tf_op jit(solution)/shard_map/rlk,kc->rlc/dot_general | solution.py:57
  402.4 0.1 slice_bitcast_fusion
  402.5 0.4 fusion.38
  402.9 0.0 copy-start.9
  402.9 3.5 fusion.24
  406.4 0.0 copy-done.9
  406.4 0.0 copy-start.1
  406.4 45.4 %fusion.32 = f32[2,256,2048]{2,0,1:T(2,128)S(1)} fusion(f32[2,256,2048]{2,1,0:T(8,128)S(1)} %fusion.24, f32[128,1,2048]{2,0,1:T(8,128)S(1)} %bitcast.33), kind=kOutput, calls=%fused_computation.47 | convolution fusion | flops 1211105280 | bytes 9437184 | tf_op jit(solution)/shard_map/conv_general_dilated | solution.py:20
  451.8 4.1 fusion.31
  455.9 0.0 copy-done.1
  (4 shorter events, 0.1 us)
Async XLA Ops:
  0.0 11.7 %copy-start = (bf16[2,32,2048]{2,1,0:T(8,128)(2,1)S(1)}, bf16[2,32,2048]{2,1,0:T(8,128)(2,1)}, u32[]{:S(2)}) copy-start(bf16[2,32,2048]{2,1,0:T(8,128)(2,1)} %param.10) | copy-start | bytes 786436
  0.0 11.7 %copy-start.12 = (s32[2,32]{1,0:T(2,128)S(1)}, s32[2,32]{1,0:T(2,128)}, u32[]{:S(2)}) copy-start(s32[2,32]{1,0:T(2,128)} %param.11) | copy-start | bytes 772
  1.2 11.4 %copy-start.6 = (bf16[256,2048]{1,0:T(8,128)(2,1)S(1)}, bf16[256,2048]{1,0:T(8,128)(2,1)}, u32[]{:S(2)}) copy-start(bf16[256,2048]{1,0:T(8,128)(2,1)} %param.9) | copy-start | bytes 3145732
  12.6 110.5 %copy-start.2 = (bf16[2,256,2048]{2,1,0:T(8,128)(2,1)}, bf16[2,256,2048]{2,1,0:T(8,128)(2,1)S(1)}, u32[]{:S(2)}) copy-start(bf16[2,256,2048]{2,1,0:T(8,128)(2,1)S(1)} %add_convert_fusion.1) | copy-start | bytes 6291460
  13.0 6.3 %copy-start.10 = (f32[128,2048]{1,0:T(8,128)S(1)}, f32[128,2048]{1,0:T(8,128)}, u32[]{:S(2)}) copy-start(f32[128,2048]{1,0:T(8,128)} %rev.6) | copy-start | bytes 3145732
  19.4 103.7 %copy-start.7 = (bf16[256,2048]{1,0:T(8,128)(2,1)S(1)}, bf16[256,2048]{1,0:T(8,128)(2,1)}, u32[]{:S(2)}) copy-start(bf16[256,2048]{1,0:T(8,128)(2,1)} %param.9) | copy-start | bytes 3145732
  123.1 150.2 %copy-start.13 = (s32[2,2]{1,0:T(2,128)S(1)}, s32[2,2]{1,0:T(2,128)}, u32[]{:S(2)}) copy-start(s32[2,2]{1,0:T(2,128)} %param.12) | copy-start | bytes 52
  123.1 159.1 %copy-start.11 = (f32[7,2048]{1,0:T(8,128)S(1)}, f32[7,2048]{1,0:T(8,128)}, u32[]{:S(2)}) copy-start(f32[7,2048]{1,0:T(8,128)} %param.16) | copy-start | bytes 172036
  127.2 73.2 %collective-permute-start = (bf16[3,256,2048]{2,1,0:T(8,128)(2,1)S(1)}, bf16[3,256,2048]{2,1,0:T(8,128)(2,1)S(1)}, u32[]{:S(2)}, u32[]{:S(2)}) collective-permute-start(bf16[3,256,2048]{2,1,0:T(8,128)(2,1)S(1)} %fusion.17), channel_id=1, source_target_pairs={{0,1},{1,2},{2,3},{3,0},{4,5},{5,6},{6,7},{7,4},{8,9},{9,10},{10,1... | collective-permute-start | bytes 9437192 | tf_op jit(solution)/shard_map/ppermute | solution.py:52
  200.4 1.6 copy-start.4
  202.1 71.2 %collective-permute-start.1 = (bf16[3,256,2048]{2,1,0:T(8,128)(2,1)S(1)}, bf16[3,256,2048]{2,1,0:T(8,128)(2,1)}, u32[]{:S(2)}, u32[]{:S(2)}) collective-permute-start(bf16[3,256,2048]{2,1,0:T(8,128)(2,1)S(1)} %collective-permute-done), channel_id=1, source_target_pairs={{0,1},{1,2},{2,3},{3,0},{4,5},{5,6},{6,7},{7,4},{8,9},{9,10},{10,1... | collective-permute-start | bytes 9437192 | tf_op jit(solution)/shard_map/ppermute | solution.py:52
  273.3 70.5 %collective-permute-start.2 = (bf16[3,256,2048]{2,1,0:T(8,128)(2,1)}, bf16[3,256,2048]{2,1,0:T(8,128)(2,1)}, u32[]{:S(2)}, u32[]{:S(2)}) collective-permute-start(bf16[3,256,2048]{2,1,0:T(8,128)(2,1)} %collective-permute-done.1), channel_id=1, source_target_pairs={{0,1},{1,2},{2,3},{3,0},{4,5},{5,6},{6,7},{7,4},{8,9},{9,10},{10,1... | collective-permute-start | bytes 9437192 | tf_op jit(solution)/shard_map/ppermute | solution.py:52
  347.7 4.1 copy-start.5
  365.7 2.6 copy-start.3
  365.7 3.0 copy-start.8
  402.9 3.5 copy-start.9
  406.4 49.5 %copy-start.1 = (bf16[2,32,2048]{2,1,0:T(8,128)(2,1)S(1)}, bf16[2,32,2048]{2,1,0:T(8,128)(2,1)}, u32[]{:S(2)}) copy-start(bf16[2,32,2048]{2,1,0:T(8,128)(2,1)} %param.10) | copy-start | bytes 786436
